TPU v7x, 32 devices: a whole 2x2x4 slice. The times are simulated.
32 devices in a mesh: seq: 8 (over z, core), head: 4 (over y, x).
Axes of the slice: x: 2, y: 2, z: 4, core: 2. Of those that a mesh axis runs over, the one named last changes fastest.
Arguments:
- x_in: bfloat16 [8192, 8192], P('seq', 'head'), may hold values from -6 to 6
- z_gate: bfloat16 [8192, 8192], P('seq', 'head'), may hold values from -6 to 6
- b_in: bfloat16 [8192, 128], P('seq'), may hold values from -6.5 to 6.5
- c_in: bfloat16 [8192, 128], P('seq'), may hold values from -6 to 6
- dt_raw: float32 [8192, 128], P('seq', 'head'), may hold values from -7.5 to 132.072
- a_log: float32 [128], P('head'), may hold values from -12 to 3.5, as said below
- d_skip: float32 [128], P('head'), may hold values from 0.5 to 1.5
- conv_x: float32 [4, 8192], P(None, 'head'), may hold values from -3 to 3
- conv_bc: float32 [4, 256], replicated, may hold values from -0.8 to 0.8
- norm_gain: float32 [8192], P('head'), may hold values from 0.1 to 1.9
- w_out: bfloat16 [8192, 4096], P('head'), may hold values from -0.0625 to 0.0625
Outputs:
- mixed: bfloat16 [8192, 4096], P(('seq', 'head'))
Inputs may be any that keep to these rules, and one draw needn't show every extreme that they name: `a_log`: logarithm of each head's decay rate.
All inputs are finite; a program needn't handle non-finite values.
Results may differ from a plain program's by a relative error of at most 0.018.
Values may be sent and summed in bfloat16 or wider, within the bound.
A program may use at most 128 MiB of HBM per device.

v0:
```python
import jax
import jax.numpy as jnp
from jax import lax
from jax.sharding import PartitionSpec as P

HEAD_DIM = 64
SPAN = 256
INNER = 8192


norm_eps = 1e-05


def passed_along(block, axis, distance):
    devices = range(lax.axis_size(axis))
    route = [(i - distance, i) for i in devices if i - distance in devices]
    return lax.ppermute(block, axis, route)


def causal_conv(values, rim, weight):
    n_rows = values.shape[0]
    padded = jnp.concatenate([rim.astype(jnp.float32), values.astype(jnp.float32)], axis=0)
    result = weight[0][None, :] * padded[0:n_rows]
    for offset in range(1, weight.shape[0]):
        result = result + weight[offset][None, :] * padded[offset : offset + n_rows]
    return jax.nn.silu(result).astype(jnp.bfloat16)


def span_step(memory, pieces):
    x_part, b_part, c_part, step_part, decay_part = pieces
    running = jnp.cumsum(decay_part, axis=0)
    length = x_part.shape[0]
    positions = lax.iota(jnp.int32, length)
    causal = positions[:, None] >= positions[None, :]
    spread = jnp.where(causal[:, :, None], running[:, None, :] - running[None, :, :], -1e30)
    scores = jnp.dot(c_part, b_part.T, preferred_element_type=jnp.float32)
    b_wide = b_part.astype(jnp.float32)
    c_wide = c_part.astype(jnp.float32)
    mixing = jnp.exp(spread) * scores[:, :, None] * step_part[None, :, :]
    inside = jnp.einsum("ijh,jhp->ihp", mixing, x_part, precision=lax.Precision.HIGHEST)
    earlier = (
        jnp.einsum("in,hpn->ihp", c_wide, memory, precision=lax.Precision.HIGHEST)
        * jnp.exp(running)[:, :, None]
    )
    final_decay = running[length - 1]
    weights = jnp.exp(final_decay[None, :] - running) * step_part
    update = jnp.einsum(
        "jhp,jn->hpn", x_part * weights[:, :, None], b_wide, precision=lax.Precision.HIGHEST
    )
    new_memory = memory * jnp.exp(final_decay)[:, None, None] + update
    return (new_memory, inside + earlier)


def local(x_in, z_gate, b_in, c_in, dt_raw, a_log, d_skip, conv_x, conv_bc, norm_gain, w_out):
    n_rows = x_in.shape[0]
    rim_rows = conv_x.shape[0] - 1
    state_size = b_in.shape[1]
    head_count = dt_raw.shape[1]
    bc_in = jnp.concatenate([b_in, c_in], axis=1)
    x_rim, bc_rim = passed_along((x_in[n_rows - rim_rows :], bc_in[n_rows - rim_rows :]), "seq", 1)
    x_conv = causal_conv(x_in, x_rim, conv_x)
    bc_conv = causal_conv(bc_in, bc_rim, conv_bc)
    b_conv = bc_conv[:, :state_size]
    c_conv = bc_conv[:, state_size:]
    dt_step = jax.nn.softplus(dt_raw)
    log_decay = -jnp.exp(a_log)[None, :] * dt_step
    x_heads = x_conv.astype(jnp.float32).reshape(n_rows, head_count, HEAD_DIM)
    blocks = n_rows // SPAN

    def split_blocks(values):
        return values.reshape((blocks, SPAN) + values.shape[1:])

    start = jnp.zeros((head_count, HEAD_DIM, state_size), jnp.float32)
    final_state, outputs = lax.scan(
        span_step,
        start,
        (
            split_blocks(x_heads),
            split_blocks(b_conv),
            split_blocks(c_conv),
            split_blocks(dt_step),
            split_blocks(log_decay),
        ),
    )
    total_decay = jnp.sum(log_decay, axis=0)
    all_decay, all_state = (
        lax.all_gather(total_decay[None].astype(jnp.bfloat16), "seq", axis=0, tiled=True).astype(
            jnp.float32
        ),
        lax.all_gather(final_state[None].astype(jnp.bfloat16), "seq", axis=0, tiled=True).astype(
            jnp.float32
        ),
    )
    my_index = lax.axis_index("seq")
    sources = lax.iota(jnp.int32, all_decay.shape[0])
    earlier_rows = (sources < my_index)[:, None]
    before_me = jnp.sum(jnp.where(earlier_rows, all_decay, 0.0), axis=0)
    upto = jnp.cumsum(all_decay, axis=0)
    exponent = jnp.where(earlier_rows, before_me[None, :] - upto, 0.0)
    factors = jnp.where(earlier_rows, jnp.exp(exponent), 0.0)
    incoming = jnp.einsum("jh,jhpn->hpn", factors, all_state, precision=lax.Precision.HIGHEST)
    inside_segment = jnp.cumsum(log_decay, axis=0)
    carried = (
        jnp.einsum(
            "ln,hpn->lhp", c_conv.astype(jnp.float32), incoming, precision=lax.Precision.HIGHEST
        )
        * jnp.exp(inside_segment)[:, :, None]
    )
    ssd = outputs.reshape(n_rows, head_count, HEAD_DIM) + carried + d_skip[None, :, None] * x_heads
    gated = ssd.reshape(n_rows, head_count * HEAD_DIM) * jax.nn.silu(z_gate.astype(jnp.float32))
    squares = lax.psum(jnp.sum(gated * gated, axis=1), "head")
    normed = (gated * lax.rsqrt(squares / INNER + norm_eps)[:, None] * norm_gain[None, :]).astype(
        jnp.bfloat16
    )
    return lax.psum_scatter(
        jnp.dot(normed, w_out, preferred_element_type=jnp.float32).astype(jnp.bfloat16),
        "head",
        scatter_dimension=0,
        tiled=True,
    )


def solution(mesh):
    in_specs = (
        P("seq", "head"),
        P("seq", "head"),
        P("seq", None),
        P("seq", None),
        P("seq", "head"),
        P("head"),
        P("head"),
        P(None, "head"),
        P(),
        P("head"),
        P("head", None),
    )
    out_specs = P(("seq", "head"), None)
    return jax.shard_map(local, mesh=mesh, in_specs=in_specs, out_specs=out_specs, check_vma=False)
```

profile of v0, /device:TPU:25, one launch (start us, length us, event | category | flops | bytes accessed | tf_op | source)
XLA Modules:
  0.0 553.7 jit_solution(4311882792378760059)
XLA Ops:
  7.3 1.3 collective-permute-start
  10.6 1.3 collective-permute-start.1
  13.6 1.1 fusion.71
  15.6 6.5 %convert_element_type.58 = f32[1024,2048]{1,0:T(8,128)} convert(bf16[1024,2048]{1,0:T(8,128)(2,1)} %param.13) | non-fusion elementwise | flops 2097152 | bytes 12582912 | tf_op jit(solution)/shard_map/convert_element_type | solution.py:22
  25.7 19.7 %fusion.58 = f32[1024,2048]{1,0:T(8,128)} fusion(f32[1024,2048]{1,0:T(8,128)} %convert_element_type.58, f32[2048]{0:T(1024)S(1)} %bitcast.144, f32[3,2048]{1,0:T(4,128)S(1)} %convert_element_type.57, f32[2048]{0:T(1024)S(1)} %bitcast.145, f32[2048]{0:T(1024)S(1)} %bitcast.143, f32[2048]{0:T(1024)S(1)} %bitcast.142), kind=kLoop, calls=%fused_computation.78 | loop fusion | flops 33554432 | bytes 16834560 | tf_op jit(solution)/shard_map/convert_element_type | solution.py:67
  45.4 14.4 %reshape.110 = f32[4,256,32,64]{3,2,1,0:T(8,128)} reshape(f32[1024,2048]{1,0:T(8,128)} %fusion.58) | data formatting | bytes 16777216 | tf_op jit(solution)/shard_map/reshape;reshape | solution.py:71
  59.9 14.2 %copy.57 = f32[4,256,32,64]{1,3,2,0:T(8,128)} copy(f32[4,256,32,64]{3,2,1,0:T(8,128)} %reshape.110) | data formatting | bytes 16777216
  74.1 265.9 %while.13 = (s32[]{:T(128)}, f32[32,64,128]{2,1,0:T(8,128)S(1)}, f32[4,256,32,64]{1,0,3,2:T(4,128)}, f32[4,256,32]{1,0,2:T(4,128)}, f32[4,256,32,64]{1,3,2,0:T(8...) while((s32[]{:T(128)}, f32[32,64,128]{2,1,0:T(8,128)S(1)}, ...), condition=%wide.region_3.4_spmd.clone, body=%wide.region_0.3_spmd.clone.sunk | while | flops 3250151424 | bytes 23631384 | solution.py:74
  74.1 1.0 constant_dynamic-slice_fusion.3
  77.4 11.1 %fusion.102 = f32[32,64,256]{2,1,0:T(8,128)S(1)} fusion(f32[256,32]{0,1:T(8,128)S(1)} %bitcast.138, f32[256,256]{1,0:T(8,128)S(1)} %fusion.101, f32[256,32]{0,1:T(8,128)S(1)} %bitcast_bitcast_fusion.3, pred[256,256]{1,0:T(8,128)(4,1)S(1)} %iota_compare_fusion.3, f32[4,256,32,64]{1,3,2,0:T(8,128)} %get-tuple-element.225, s32[]{:T(128)S(6)} %copy.116), kind=kOutput, calls=%fused_computation.clone.1 | convolution fusion | flops 1619001344 | bytes 4620292 | tf_op jit(solution)/shard_map/while/body/eval_jaxpr/ijh,jhp->ihp/dot_general | solution.py:40
  88.5 1.1 fusion.103
  89.6 2.2 copy.110
  91.7 3.2 fusion.100
  94.9 45.6 %dynamic_update_slice.6 = f32[4,256,32,64]{1,0,3,2:T(4,128)} dynamic-update-slice(f32[4,256,32,64]{1,0,3,2:T(4,128)} %get-tuple-element.212, f32[1,256,32,64]{1,0,3,2:T(1,128)S(1)} %copy.110, s32[]{:T(128)S(6)} %copy.116, s32[]{:T(128)} %constant.45.clone.1..sunk, s32[]{:T(128)} %constant.45.clone.1..sunk, s32[]{:T(128)} %constant.45.clone.1..sunk) | dynamic-update-slice | bytes 4194308 | tf_op jit(solution)/shard_map/while/body/jit(dynamic_update_index_in_dim)/dynamic_update_slice | solution.py:74
  140.6 1.0 constant_dynamic-slice_fusion.3
  142.8 1.0 fusion.101
  143.9 11.1 %fusion.102 = f32[32,64,256]{2,1,0:T(8,128)S(1)} fusion(f32[256,32]{0,1:T(8,128)S(1)} %bitcast.138, f32[256,256]{1,0:T(8,128)S(1)} %fusion.101, f32[256,32]{0,1:T(8,128)S(1)} %bitcast_bitcast_fusion.3, pred[256,256]{1,0:T(8,128)(4,1)S(1)} %iota_compare_fusion.3, f32[4,256,32,64]{1,3,2,0:T(8,128)} %get-tuple-element.225, s32[]{:T(128)S(6)} %copy.116), kind=kOutput, calls=%fused_computation.clone.1 | convolution fusion | flops 1619001344 | bytes 4620292 | tf_op jit(solution)/shard_map/while/body/eval_jaxpr/ijh,jhp->ihp/dot_general | solution.py:40
  155.0 1.1 fusion.103
  156.1 2.2 copy.110
  158.2 3.2 fusion.100
  161.4 45.6 %dynamic_update_slice.6 = f32[4,256,32,64]{1,0,3,2:T(4,128)} dynamic-update-slice(f32[4,256,32,64]{1,0,3,2:T(4,128)} %get-tuple-element.212, f32[1,256,32,64]{1,0,3,2:T(1,128)S(1)} %copy.110, s32[]{:T(128)S(6)} %copy.116, s32[]{:T(128)} %constant.45.clone.1..sunk, s32[]{:T(128)} %constant.45.clone.1..sunk, s32[]{:T(128)} %constant.45.clone.1..sunk) | dynamic-update-slice | bytes 4194308 | tf_op jit(solution)/shard_map/while/body/jit(dynamic_update_index_in_dim)/dynamic_update_slice | solution.py:74
  207.1 1.0 constant_dynamic-slice_fusion.3
  209.3 1.0 fusion.101
  210.4 11.1 %fusion.102 = f32[32,64,256]{2,1,0:T(8,128)S(1)} fusion(f32[256,32]{0,1:T(8,128)S(1)} %bitcast.138, f32[256,256]{1,0:T(8,128)S(1)} %fusion.101, f32[256,32]{0,1:T(8,128)S(1)} %bitcast_bitcast_fusion.3, pred[256,256]{1,0:T(8,128)(4,1)S(1)} %iota_compare_fusion.3, f32[4,256,32,64]{1,3,2,0:T(8,128)} %get-tuple-element.225, s32[]{:T(128)S(6)} %copy.116), kind=kOutput, calls=%fused_computation.clone.1 | convolution fusion | flops 1619001344 | bytes 4620292 | tf_op jit(solution)/shard_map/while/body/eval_jaxpr/ijh,jhp->ihp/dot_general | solution.py:40
  221.5 1.1 fusion.103
  222.6 2.2 copy.110
  224.7 3.2 fusion.100
  227.9 45.6 %dynamic_update_slice.6 = f32[4,256,32,64]{1,0,3,2:T(4,128)} dynamic-update-slice(f32[4,256,32,64]{1,0,3,2:T(4,128)} %get-tuple-element.212, f32[1,256,32,64]{1,0,3,2:T(1,128)S(1)} %copy.110, s32[]{:T(128)S(6)} %copy.116, s32[]{:T(128)} %constant.45.clone.1..sunk, s32[]{:T(128)} %constant.45.clone.1..sunk, s32[]{:T(128)} %constant.45.clone.1..sunk) | dynamic-update-slice | bytes 4194308 | tf_op jit(solution)/shard_map/while/body/jit(dynamic_update_index_in_dim)/dynamic_update_slice | solution.py:74
  273.6 1.0 constant_dynamic-slice_fusion.3
  275.8 1.0 fusion.101
  276.9 11.1 %fusion.102 = f32[32,64,256]{2,1,0:T(8,128)S(1)} fusion(f32[256,32]{0,1:T(8,128)S(1)} %bitcast.138, f32[256,256]{1,0:T(8,128)S(1)} %fusion.101, f32[256,32]{0,1:T(8,128)S(1)} %bitcast_bitcast_fusion.3, pred[256,256]{1,0:T(8,128)(4,1)S(1)} %iota_compare_fusion.3, f32[4,256,32,64]{1,3,2,0:T(8,128)} %get-tuple-element.225, s32[]{:T(128)S(6)} %copy.116), kind=kOutput, calls=%fused_computation.clone.1 | convolution fusion | flops 1619001344 | bytes 4620292 | tf_op jit(solution)/shard_map/while/body/eval_jaxpr/ijh,jhp->ihp/dot_general | solution.py:40
  287.9 1.1 fusion.103
  289.0 2.2 copy.110
  291.2 3.2 fusion.100
  294.4 45.6 %dynamic_update_slice.6 = f32[4,256,32,64]{1,0,3,2:T(4,128)} dynamic-update-slice(f32[4,256,32,64]{1,0,3,2:T(4,128)} %get-tuple-element.212, f32[1,256,32,64]{1,0,3,2:T(1,128)S(1)} %copy.110, s32[]{:T(128)S(6)} %copy.116, s32[]{:T(128)} %constant.45.clone.1..sunk, s32[]{:T(128)} %constant.45.clone.1..sunk, s32[]{:T(128)} %constant.45.clone.1..sunk) | dynamic-update-slice | bytes 4194308 | tf_op jit(solution)/shard_map/while/body/jit(dynamic_update_index_in_dim)/dynamic_update_slice | solution.py:74
  342.5 13.3 %all-reduce = bf16[256]{0:T(256)(128)(2,1)S(1)} all-reduce(bf16[256]{0:T(256)(128)(2,1)S(1)} %dynamic-update-slice), channel_id=2, replica_groups=mesh['seq'=8,'head'=4] {'seq'}, use_global_device_ids=true, to_apply=%add | all-reduce | flops 256 | bytes 1024
  356.1 9.0 %reduce-window.16 = f32[32,8,128]{2,1,0:T(8,128)S(1)} reduce-window(f32[32,8,128]{2,1,0:T(8,128)S(1)} %bitcast.141, f32[]{:T(128)} %constant.46.clone.1), window={size=1x1x128 pad=0_0x0_0x127_0}, to_apply=%region_7.8 | reduce-window | flops 4161536 | bytes 262148 | tf_op jit(solution)/shard_map/reduce-window.2
  365.6 9.3 %copy.62 = f32[1024,2048]{0,1:T(8,128)} copy(f32[1024,2048]{1,0:T(8,128)} %fusion.58) | data formatting | bytes 16777216 | tf_op jit(solution)/shard_map/convert_element_type | solution.py:67
  374.9 10.9 %reshape.90 = f32[1024,32,64]{0,2,1:T(8,128)} reshape(f32[4,256,32,64]{1,0,3,2:T(4,128)} %get-tuple-element.48) | data formatting | bytes 16777216 | tf_op jit(solution)/shard_map/reshape | solution.py:109
  385.8 3.7 all-gather.4.cloned.1.call-done
  389.5 7.3 %fusion.54 = f32[32,1,64,128]{3,1,2,0:T(1,128)S(1)} fusion(f32[8,32,1,1]{0,2,3,1:T(1,128)S(1)} %copy.64, bf16[8,32,64,128]{3,2,1,0:T(8,128)(2,1)} %bitcast.135), kind=kOutput, calls=%fused_computation.74 | convolution fusion | flops 25165824 | bytes 5243904 | tf_op jit(solution)/shard_map/jh,jhpn->hpn/dot_general | solution.py:101
  396.8 3.5 fusion.67
  400.4 7.4 %multiply_add_fusion = f32[1024,32,64]{0,2,1:T(8,128)} fusion(f32[1024,32,64]{0,2,1:T(8,128)S(1)} %bitcast.132, f32[1024,32,64]{0,2,1:T(8,128)} %reshape.90, f32[1024,32,64]{0,2,1:T(8,128)S(1)} %fusion.67, f32[32]{0:T(128)S(1)} %copy-done.2, f32[1024,32]{0,1:T(8,128)S(1)} %bitcast.139), kind=kLoop, calls=%fused_computation.71 | loop fusion | flops 8388608 | bytes 33685632 | tf_op jit(solution)/shard_map/add | solution.py:109
  407.8 9.1 %copy.63 = f32[1024,2048]{1,0:T(8,128)} copy(f32[1024,2048]{0,1:T(8,128)} %bitcast.133) | data formatting | bytes 16777216 | tf_op jit(solution)/shard_map/reshape | solution.py:110
  416.9 6.0 %multiply_reduce_fusion = f32[1024]{0:T(1024)S(1)} fusion(f32[1024,2048]{1,0:T(8,128)} %copy.63, bf16[1024,2048]{1,0:T(8,128)(2,1)} %param.14), kind=kLoop, calls=%fused_computation.70 | loop fusion | flops 16776192 | bytes 12587008 | tf_op jit(solution)/shard_map/reduce_sum | solution.py:111
  423.0 7.8 %psum.7 = f32[1024]{0:T(1024)S(1)} all-reduce(f32[1024]{0:T(1024)S(1)} %multiply_reduce_fusion), channel_id=1, replica_groups=mesh['seq'=8,'head'=4] {'head'}, use_global_device_ids=true, to_apply=%region_10.11 | all-reduce | flops 1024 | bytes 8192 | tf_op jit(solution)/shard_map/psum | solution.py:111
  430.8 28.8 %convolution_convert_fusion = bf16[1024,4096]{1,0:T(8,128)(2,1)} fusion(bf16[2048,4096]{1,0:T(8,128)(2,1)} %param.23, f32[2048]{0:T(1024)S(1)} %copy-done.3, f32[1024]{0:T(1024)S(1)} %add_rsqrt_fusion, f32[1024,2048]{1,0:T(8,128)} %copy.63, bf16[1024,2048]{1,0:T(8,128)(2,1)} %param.14), kind=kOutput, calls=%fused_computation.73 | convolution fusion | flops 17202937856 | bytes 37761024 | tf_op jit(solution)/shard_map/dot_general | solution.py:116
  459.6 87.2 %reduce-scatter.2.cloned.1.call-done = bf16[256,4096]{1,0:T(8,128)(2,1)} async-done(((bf16[1024,4096]{1,0:T(8,128)(2,1)}), bf16[256,4096]{1,0:T(8,128)(2,1)}) %reduce-scatter.2.cloned.1.call-update) | async-done | bytes 2097168 | tf_op jit(solution)/shard_map/reduce_scatter | solution.py:115
  (101 shorter events, 17.4 us)
Async XLA Ops:
  6.5 383.0 %all-gather.4.cloned.1.call-start = ((), (), s32[]{:S(2)}) async-start(), calls=%async_computation.2 | async-start | bytes 4718592 | tf_op jit(solution)/shard_map/all_gather | solution.py:90
  7.3 18.4 %collective-permute-start = (bf16[3,2048]{1,0:T(4,128)(2,1)S(1)}, bf16[3,2048]{1,0:T(4,128)(2,1)S(1)}, u32[]{:S(2)}, u32[]{:S(2)}) collective-permute-start(bf16[3,2048]{1,0:T(4,128)(2,1)S(1)} %slice.70), channel_id=1, source_target_pairs={{0,4},{4,8},{8,12},{12,16},{16,20},{20,24},{24,28},{1,5},{5,9},{9,... | collective-permute-start | bytes 36872 | tf_op jit(solution)/shard_map/ppermute | solution.py:17
  10.6 12.8 %collective-permute-start.1 = (bf16[3,256]{1,0:T(4,128)(2,1)S(1)}, bf16[3,256]{1,0:T(4,128)(2,1)S(1)}, u32[]{:S(2)}, u32[]{:S(2)}) collective-permute-start(bf16[3,256]{1,0:T(4,128)(2,1)S(1)} %slice.98), channel_id=1, source_target_pairs={{0,4},{4,8},{8,12},{12,16},{16,20},{20,24},{24,28},{1,5},{5,9},{9,... | collective-permute-start | bytes 4616 | tf_op jit(solution)/shard_map/ppermute | solution.py:17
  24.1 0.8 copy-start
  74.1 266.9 %copy-start.4 = (u32[32]{0:T(128)S(1)}, u32[32]{0:T(128)}, u32[]{:S(2)}) copy-start(u32[32]{0:T(128)} %constant.54) | copy-start | bytes 388
  340.9 205.9 %reduce-scatter.2.cloned.1.call-start = ((), (), s32[]{:S(2)}) async-start(), calls=%async_computation.1 | async-start | bytes 10485760 | tf_op jit(solution)/shard_map/reduce_scatter | solution.py:115
  374.9 21.9 %copy-start.1 = (bf16[1024,256]{1,0:T(8,128)(2,1)S(1)}, bf16[1024,256]{1,0:T(8,128)(2,1)}, u32[]{:S(2)}) copy-start(bf16[1024,256]{1,0:T(8,128)(2,1)} %copy-done) | copy-start | bytes 1572868
  389.5 10.8 %slice-start = ((s8[8388608]{0:T(1024)(128)(4,1)}), s8[4194304]{0:T(1024)(128)(4,1)S(1)}, s32[]{:S(2)}) async-start(s8[8388608]{0:T(1024)(128)(4,1)} %bitcast.130), calls=%async_computation.3 | async-start | bytes 8388608
  389.5 10.8 %copy-start.2 = (f32[32]{0:T(128)S(1)}, f32[32]{0:T(128)}, u32[]{:S(2)}) copy-start(f32[32]{0:T(128)} %param.19) | copy-start | bytes 388
  396.8 3.5 slice-start.1
  416.9 13.9 %copy-start.3 = (f32[2048]{0:T(1024)S(1)}, f32[2048]{0:T(1024)}, u32[]{:S(2)}) copy-start(f32[2048]{0:T(1024)} %param.22) | copy-start | bytes 24580
Sparse Core Ops, SparseCore 0:
  341.0 48.4 all-gather.3
  459.7 87.0 reduce-scatter.1
where the time goes:
time: 562 us; the launch traced here: 554 us
  local copies, waits for them, and re-layouts  264 us (47%)
  matrix products  105 us (19%)
  waiting for transfers between devices  91 us (16%)
  other arithmetic  55.8 us (10%)
  blocking collectives  21.1 us (4%)
  between operations  14.2 us (3%)
    dynamic_update_slice x8, local copies, waits for them, and re-layouts, local(): lax.scan(span_step, start, (split_blocks(x_heads), split_blocks(b_conv),...  191 us
    reduce_scatter x1, waiting for transfers between devices, local(): lax.psum_scatter(jnp.dot(normed, w_out, preferred_element_type=jnp.float3...  87.2 us
    dot_general x4, matrix products, span_step(): jnp.einsum('ijh,jhp->ihp', mixing, x_part, precision=lax.Precision.HIGHEST)  44.3 us
    dot_general x1, matrix products, local(): jnp.dot(normed, w_out, preferred_element_type=jnp.float32)  28.8 us
    convert_element_type x1, other arithmetic, local(): x_heads = x_conv.astype(jnp.float32).reshape(n_rows, head_count, HEAD_DIM)  19.7 us
    unnamed x21, local copies, waits for them, and re-layouts  16.9 us
    another operation x1, local copies, waits for them, and re-layouts, split_blocks(): return values.reshape((blocks, SPAN) + values.shape[1:])  14.4 us
    unnamed x1, blocking collectives  13.3 us
  transfers between devices with their start and end apart: 4, of which 2 were waited for; matrix products, arithmetic and copies ran while one was open for 8% of the time, Pallas kernels for 0%

commit v1 on v0

v1 whole, which is shorter than its diff:
```python
import functools

import jax
import jax.numpy as jnp
from jax import lax
from jax.experimental import pallas as pl
from jax.experimental.pallas import tpu as pltpu
from jax.sharding import PartitionSpec as P

HEAD_DIM = 64
INNER = 8192
NORM_EPS = 1e-05
MESH = pl.DeviceIdType.MESH

CHUNK = 128
RIM = 16
TILE = 512
LANES = 128


def silu(v):
    return v / (1.0 + jnp.exp(-v))


def remote(src, dst, send, recv, **where):
    return pltpu.make_async_remote_copy(
        src_ref=src, dst_ref=dst, send_sem=send, recv_sem=recv, device_id=where, device_id_type=MESH
    )


def kernel(
    n_seq, n_head,
    x_hbm, z_hbm, b_hbm, c_hbm, w_hbm, dt_ref, rate_ref, skip_ref, cx_ref, cbc_ref, gain_ref,
    out_ref,
    x_v, z_v, w_v, bc_v, y_v, s_v, f_v, carry_in, carry_out, spread_v, pad_v, padbc_v,
    cs_v, dt_v, cst_v, dtt_v, tot_v, dev_v, sq_v, sq_in, send_v, mid_v, recv_v,
    load_sem, rim_send, rim_recv, carry_send, carry_recv, sq_send, sq_recv,
    out_send, mid_recv, fin_recv,
):
    rows, chans = z_v.shape
    heads = chans // HEAD_DIM
    chunks = rows // CHUNK
    own_rows = rows // n_head
    tiles = w_v.shape[1] // TILE
    pieces = carry_send.shape[0]
    piece = chans // pieces
    seq = lax.axis_index("seq")
    head = lax.axis_index("head")
    state = b_hbm.shape[1]

    loads = [
        pltpu.make_async_copy(x_hbm, x_v.at[pl.ds(RIM, rows)], load_sem.at[0]),
        pltpu.make_async_copy(b_hbm, bc_v.at[pl.ds(RIM, rows), pl.ds(0, state)], load_sem.at[1]),
        pltpu.make_async_copy(c_hbm, bc_v.at[pl.ds(RIM, rows), pl.ds(state, state)], load_sem.at[2]),
        pltpu.make_async_copy(z_hbm, z_v, load_sem.at[3]),
        pltpu.make_async_copy(w_hbm, w_v, load_sem.at[4]),
    ]
    for copy in loads:
        copy.start()

    barrier = pltpu.get_barrier_semaphore()
    for s in range(1, n_head):
        pl.semaphore_signal(barrier, inc=1, device_id={"head": lax.rem(head + s, n_head)}, device_id_type=MESH)

    for s in (1, n_seq - 1):
        pl.semaphore_signal(barrier, inc=1, device_id={"seq": lax.rem(seq + s, n_seq)}, device_id_type=MESH)
    pl.semaphore_wait(barrier, n_head + 1)

    tail = pl.ds(rows - RIM, RIM)
    rims = [
        remote(x_hbm.at[tail], x_v.at[pl.ds(0, RIM)], rim_send.at[0], rim_recv.at[0], seq=seq + 1),
        remote(b_hbm.at[tail], bc_v.at[pl.ds(0, RIM), pl.ds(0, state)], rim_send.at[1], rim_recv.at[1], seq=seq + 1),
        remote(c_hbm.at[tail], bc_v.at[pl.ds(0, RIM), pl.ds(state, state)], rim_send.at[2], rim_recv.at[2], seq=seq + 1),
    ]

    @pl.when(seq < n_seq - 1)
    def _():
        for copy in rims:
            copy.start()

    @pl.when(seq == 0)
    def _():
        x_v[0:RIM, :] = jnp.zeros((RIM, chans), jnp.bfloat16)
        bc_v[0:RIM, :] = jnp.zeros((RIM, 2 * state), jnp.bfloat16)
        carry_in[...] = jnp.zeros_like(carry_in)

    of_lane = lax.broadcasted_iota(jnp.int32, (2 * LANES, chans), 1) // HEAD_DIM
    of_row = lax.broadcasted_iota(jnp.int32, (2 * LANES, chans), 0) % LANES
    spread_v[...] = jnp.where(of_lane == of_row, 1.0, 0.0).astype(jnp.bfloat16)
    dt_v[...] = jnp.zeros_like(dt_v)
    dt_v[:, 0:heads] = dt_ref[...]
    f_v[...] = jnp.zeros_like(f_v)
    dev_v[...] = jnp.ones_like(dev_v)

    row_id = lax.broadcasted_iota(jnp.int32, (CHUNK, CHUNK), 0)
    col_id = lax.broadcasted_iota(jnp.int32, (CHUNK, CHUNK), 1)
    causal = row_id >= col_id

    def over_channels(values):
        high = values.astype(jnp.bfloat16)
        low = (values - high.astype(jnp.float32)).astype(jnp.bfloat16)
        return jnp.dot(
            jnp.concatenate([high, low], axis=1), spread_v[...], preferred_element_type=jnp.float32
        )

    def conv(values_ref, padded, start, taps):
        padded[0:8, :] = values_ref[pl.ds(start, RIM), :].astype(jnp.float32)[8:16]
        padded[8 : 8 + CHUNK, :] = values_ref[pl.ds(start + RIM, CHUNK), :].astype(jnp.float32)
        total = taps[0:1, :] * padded[5 : 5 + CHUNK, :]
        for k in range(1, 4):
            total = total + taps[k : k + 1, :] * padded[5 + k : 5 + k + CHUNK, :]
        values_ref[pl.ds(start + RIM, CHUNK), :] = silu(total).astype(jnp.bfloat16)

    for copy in loads[:3]:
        copy.wait()

    def state_step(i, _):
        c = chunks - 1 - i
        start = pl.multiple_of(c * CHUNK, CHUNK)

        @pl.when((c == 0) & (seq > 0))
        def _():
            for copy in rims:
                copy.wait_recv()

        conv(x_v, pad_v, start, cx_ref)
        conv(bc_v, padbc_v, start, cbc_ref)
        raw = dt_v[pl.ds(start, CHUNK), :]
        dt = jnp.maximum(raw, 0.0) + jnp.log1p(jnp.exp(-jnp.abs(raw)))
        decay = -jnp.exp(rate_ref[...]) * dt
        running = jnp.dot(
            jnp.where(causal, 1.0, 0.0), decay,
            precision=lax.Precision.HIGHEST, preferred_element_type=jnp.float32,
        )
        dt_v[pl.ds(start, CHUNK), :] = dt
        cs_v[pl.ds(start, CHUNK), :] = running
        cst_v[pl.ds(start, CHUNK), :] = running.T
        dtt_v[pl.ds(start, CHUNK), :] = dt.T
        last = running[CHUNK - 1 : CHUNK, :]
        end = over_channels(jnp.broadcast_to(jnp.exp(last), (8, LANES)))
        tot_v[pl.ds(pl.multiple_of(c * 8, 8), 8), :] = end
        weights = over_channels(jnp.exp(last - running) * dt)
        xw = (weights * x_v[pl.ds(start + RIM, CHUNK), :].astype(jnp.float32)).astype(jnp.bfloat16)
        b_t = bc_v[pl.ds(start + RIM, CHUNK), 0:state].astype(jnp.float32).T.astype(jnp.bfloat16)
        update = jnp.dot(b_t, xw, preferred_element_type=jnp.float32)
        s_v[pl.ds(pl.multiple_of(c * state, state), state), :] = update.astype(jnp.bfloat16)
        f_v[...] += dev_v[0:1, :] * update
        dev_v[...] = dev_v[...] * end
        return 0

    lax.fori_loop(0, chunks, state_step, 0)

    def carry_copy(k):
        columns = pl.ds(k * piece, piece)
        return remote(
            carry_out.at[:, columns], carry_in.at[:, columns], carry_send.at[k], carry_recv.at[k], seq=seq + 1
        )

    def within(c, _):
        @pl.when(c == seq * chunks // n_seq)
        def _():
            for k in range(pieces):
                @pl.when(seq > 0)
                def _():
                    carry_copy(k).wait_recv()

                @pl.when(seq < n_seq - 1)
                def _():
                    columns = slice(k * piece, (k + 1) * piece)
                    carry_out[:, columns] = (
                        dev_v[0:1, columns] * carry_in[:, columns].astype(jnp.float32) + f_v[:, columns]
                    ).astype(jnp.bfloat16)
                    carry_copy(k).start()

        start = pl.multiple_of(c * CHUNK, CHUNK)
        b = bc_v[pl.ds(start + RIM, CHUNK), 0:state]
        cc = bc_v[pl.ds(start + RIM, CHUNK), state : 2 * state]
        scores = lax.dot_general(cc, b, (((1,), (1,)), ((), ())), preferred_element_type=jnp.float32)
        scores = jnp.where(causal, scores, 0.0)
        running = cs_v[pl.ds(start, CHUNK), :]
        across = cst_v[pl.ds(start, CHUNK), :]
        steps = dtt_v[pl.ds(start, CHUNK), :]
        left = lax.broadcasted_iota(jnp.int32, (CHUNK, LANES), 1) < HEAD_DIM
        zero = jnp.zeros((CHUNK, LANES), jnp.bfloat16)
        for pair in range(heads // 2):
            mixes = []
            for h in (2 * pair, 2 * pair + 1):
                gap = running[:, h : h + 1] - across[h : h + 1, :]
                mix = jnp.exp(jnp.minimum(gap, 0.0)) * (scores * steps[h : h + 1, :])
                mixes.append(mix.astype(jnp.bfloat16))
            lanes = slice(pair * LANES, (pair + 1) * LANES)
            xp = x_v[pl.ds(start + RIM, CHUNK), lanes]
            both = jnp.concatenate([jnp.where(left, xp, zero), jnp.where(left, zero, xp)], axis=0)
            y_v[pl.ds(start, CHUNK), lanes] = jnp.dot(
                jnp.concatenate(mixes, axis=1), both, preferred_element_type=jnp.float32
            )
        return 0

    lax.fori_loop(0, chunks, within, 0)

    f_v[...] = carry_in[...].astype(jnp.float32)

    def starts(c, _):
        here = pl.ds(pl.multiple_of(c * state, state), state)
        update = s_v[here, :].astype(jnp.float32)
        now = f_v[...]
        s_v[here, :] = now.astype(jnp.bfloat16)
        f_v[...] = now * tot_v[pl.ds(pl.multiple_of(c * 8, 8), 8), :][0:1, :] + update
        return 0

    lax.fori_loop(0, chunks, starts, 0)
    loads[3].wait()

    def gate(c):
        start = pl.multiple_of(c * CHUNK, CHUNK)
        here = pl.ds(start, CHUNK)
        cc = bc_v[pl.ds(start + RIM, CHUNK), state : 2 * state]
        grown = over_channels(jnp.exp(cs_v[here, :]))
        earlier = jnp.dot(
            cc, s_v[pl.ds(pl.multiple_of(c * state, state), state), :], preferred_element_type=jnp.float32
        )
        x = x_v[pl.ds(start + RIM, CHUNK), :].astype(jnp.float32)
        ssd = y_v[here, :] + earlier * grown + skip_ref[...] * x
        gated = ssd * silu(z_v[here, :].astype(jnp.float32))
        z_v[here, :] = (gated * gain_ref[...]).astype(jnp.bfloat16)
        squares = gated * gated
        total = squares[:, 0:LANES]
        for g in range(1, chans // LANES):
            total = total + squares[:, g * LANES : (g + 1) * LANES]
        sq_v[here, :] = total

    def product(block, t):
        columns = pl.ds(pl.multiple_of(t * TILE, TILE), TILE)
        here = pl.ds(pl.multiple_of(block * own_rows, own_rows), own_rows)
        return jnp.dot(z_v[here, :], w_v[:, columns], preferred_element_type=jnp.float32)

    def sq_copy(s):
        target = lax.rem(head + s, n_head)
        here = pl.ds(pl.multiple_of(target * own_rows, own_rows), own_rows)
        return remote(sq_v.at[here], sq_in.at[s - 1], sq_send.at[s - 1], sq_recv.at[s - 1], head=target)

    def finish(slots):
        here = pl.ds(pl.multiple_of(head * own_rows, own_rows), own_rows)
        squares = sq_v[here, :]
        for s in range(1, n_head):
            sq_copy(s).wait_recv()
            squares = squares + sq_in[s - 1]
        scale = lax.rsqrt(jnp.sum(squares, axis=1, keepdims=True) / INNER + NORM_EPS)
        sq_v[here, :] = jnp.broadcast_to(scale, (own_rows, LANES))

        def last(t, _):
            total = product(head, t)
            for slot in range(slots):
                fin_copy(slot, t).wait_recv()
                total = total + recv_v[slot, t].astype(jnp.float32)
            columns = pl.ds(pl.multiple_of(t * TILE, TILE), TILE)
            scale = sq_v[here, :][:, 0:1]
            out_ref[:, columns] = (total * scale).astype(jnp.bfloat16)
            return 0

        lax.fori_loop(0, tiles, last, 0)

    if n_head == 4:
        by_x = head + 1 - 2 * lax.rem(head, 2)
        by_y = lax.rem(head + 2, 4)
        far = 3 - head
        half = tiles // 2
        per_block = own_rows // CHUNK

        def gates(block):
            lax.fori_loop(0, per_block, lambda i, _: (gate(block * per_block + i), 0)[1], 0)

        def mid_copy(t, target):
            return remote(send_v.at[0, t], mid_v.at[t], out_send.at[0, t], mid_recv.at[t], head=target)

        def fin_copy(slot, t):
            return remote(
                send_v.at[slot + 1, t], recv_v.at[slot, t], out_send.at[slot + 1, t], fin_recv.at[slot, t],
                head=by_x if slot == 0 else by_y,
            )

        gates(far)
        loads[4].wait()

        def first(i, _):
            send_v[0, i] = product(far, i).astype(jnp.bfloat16)
            mid_copy(i, by_x).start()
            send_v[0, i + half] = product(far, i + half).astype(jnp.bfloat16)
            mid_copy(i + half, by_y).start()
            return 0

        lax.fori_loop(0, half, first, 0)
        gates(by_x)
        gates(by_y)

        def plain(i, _):
            send_v[1, i] = product(by_x, i).astype(jnp.bfloat16)
            fin_copy(0, i).start()
            send_v[2, i + half] = product(by_y, i + half).astype(jnp.bfloat16)
            fin_copy(1, i + half).start()
            return 0

        lax.fori_loop(0, half, plain, 0)
        gates(head)
        for s in range(1, n_head):
            sq_copy(s).start()

        def relayed(i, _):
            mine = product(by_x, i + half)
            mid_copy(i + half, by_y).wait_recv()
            send_v[1, i + half] = (mine + mid_v[i + half].astype(jnp.float32)).astype(jnp.bfloat16)
            fin_copy(0, i + half).start()
            mine = product(by_y, i)
            mid_copy(i, by_x).wait_recv()
            send_v[2, i] = (mine + mid_v[i].astype(jnp.float32)).astype(jnp.bfloat16)
            fin_copy(1, i).start()
            return 0

        lax.fori_loop(0, half, relayed, 0)
        finish(2)

        def sent(t, _):
            fin_copy(0, t).wait_send()
            fin_copy(1, t).wait_send()
            mid_copy(t, by_x).wait_send()
            return 0

        lax.fori_loop(0, tiles, sent, 0)
    else:
        def fin_copy(slot, t):
            return remote(
                send_v.at[slot, t], recv_v.at[slot, t], out_send.at[slot, t], fin_recv.at[slot, t],
                head=lax.rem(head + slot + 1, n_head),
            )

        lax.fori_loop(0, chunks, lambda c, _: (gate(c), 0)[1], 0)
        loads[4].wait()
        for s in range(1, n_head):
            sq_copy(s).start()

        def each(slot, _):
            def tile(t, _):
                send_v[slot, t] = product(lax.rem(head + slot + 1, n_head), t).astype(jnp.bfloat16)
                fin_copy(slot, t).start()
                return 0

            return lax.fori_loop(0, tiles, tile, 0)

        lax.fori_loop(0, n_head - 1, each, 0)
        finish(n_head - 1)

        def sent(slot, _):
            def tile(t, _):
                fin_copy(slot, t).wait_send()
                return 0

            return lax.fori_loop(0, tiles, tile, 0)

        lax.fori_loop(0, n_head - 1, sent, 0)

    for s in range(1, n_head):
        sq_copy(s).wait_send()

    @pl.when(seq < n_seq - 1)
    def _():
        for copy in rims:
            copy.wait_send()
        for k in range(pieces):
            carry_copy(k).wait_send()


def local(n_seq, n_head, x_in, z_gate, b_in, c_in, dt_raw, a_log, d_skip, conv_x, conv_bc, norm_gain, w_out):
    rows, chans = x_in.shape
    state = b_in.shape[1]
    width = w_out.shape[1]
    own = rows // n_head
    tiles = width // TILE
    chunks = rows // CHUNK
    pieces = 4
    heads = a_log.shape[0]
    rate = jnp.pad(a_log, (0, LANES - heads))[None, :]
    skip = jnp.repeat(d_skip, HEAD_DIM)[None, :]
    sends, mids, slots = (3, tiles, 2) if n_head == 4 else (n_head - 1, 1, n_head - 1)
    bf, f32 = jnp.bfloat16, jnp.float32
    any_spec = pl.BlockSpec(memory_space=pl.ANY)
    vmem = pl.BlockSpec(memory_space=pltpu.VMEM)
    dma = pltpu.SemaphoreType.DMA
    flops = 2 * rows * chans * (width + 3 * state)
    return pl.pallas_call(
        functools.partial(kernel, n_seq, n_head),
        out_shape=jax.ShapeDtypeStruct((own, width), bf),
        in_specs=[any_spec] * 5 + [vmem] * 6,
        out_specs=vmem,
        scratch_shapes=[
            pltpu.VMEM((RIM + rows, chans), bf),
            pltpu.VMEM((rows, chans), bf),
            pltpu.VMEM((chans, width), bf),
            pltpu.VMEM((RIM + rows, 2 * state), bf),
            pltpu.VMEM((rows, chans), f32),
            pltpu.VMEM((chunks * state, chans), bf),
            pltpu.VMEM((state, chans), f32),
            pltpu.VMEM((state, chans), bf),
            pltpu.VMEM((state, chans), bf),
            pltpu.VMEM((2 * LANES, chans), bf),
            pltpu.VMEM((8 + CHUNK, chans), f32),
            pltpu.VMEM((8 + CHUNK, 2 * state), f32),
            pltpu.VMEM((rows, LANES), f32),
            pltpu.VMEM((rows, LANES), f32),
            pltpu.VMEM((chunks * LANES, CHUNK), f32),
            pltpu.VMEM((chunks * LANES, CHUNK), f32),
            pltpu.VMEM((chunks * 8, chans), f32),
            pltpu.VMEM((8, chans), f32),
            pltpu.VMEM((rows, LANES), f32),
            pltpu.VMEM((n_head - 1, own, LANES), f32),
            pltpu.VMEM((sends, tiles, own, TILE), bf),
            pltpu.VMEM((mids, own, TILE), bf),
            pltpu.VMEM((slots, tiles, own, TILE), bf),
            dma((5,)), dma((3,)), dma((3,)), dma((pieces,)), dma((pieces,)),
            dma((n_head - 1,)), dma((n_head - 1,)),
            dma((sends, tiles)), dma((mids,)), dma((slots, tiles)),
        ],
        compiler_params=pltpu.CompilerParams(
            collective_id=0, has_side_effects=True, vmem_limit_bytes=62 * 1024 * 1024
        ),
        cost_estimate=pl.CostEstimate(
            flops=flops, bytes_accessed=2 * (2 * rows * chans + chans * width), transcendentals=rows * chans
        ),
    )(x_in, z_gate, b_in, c_in, w_out, dt_raw, rate, skip, conv_x, conv_bc, norm_gain[None, :])


def solution(mesh):
    in_specs = (
        P("seq", "head"), P("seq", "head"), P("seq", None), P("seq", None), P("seq", "head"),
        P("head"), P("head"), P(None, "head"), P(), P("head"), P("head", None),
    )
    body = functools.partial(local, mesh.shape["seq"], mesh.shape["head"])
    return jax.shard_map(
        body, mesh=mesh, in_specs=in_specs, out_specs=P(("seq", "head"), None), check_vma=False
    )
```

time: 562 us -> 133 us (0.24); the launches traced: 554 us -> 133 us
  local copies, waits for them, and re-layouts: 264 us -> 7.63 us
  Pallas kernels: 0 us -> 125 us
  matrix products: 105 us -> 0 us
  waiting for transfers between devices: 91 us -> 0 us
  other arithmetic: 55.8 us -> 0 us
  blocking collectives: 21.1 us -> 0 us
  between operations: 14.2 us -> 0.01 us
    dynamic_update_slice x8 -> x0, local copies, waits for them, and re-layouts: 191 us -> none  [local(): lax.scan(span_step, start, (split_blocks(x_heads), split_blocks(b_conv),...]
    pallas_call x0 -> x1, Pallas kernels: none -> 125 us  [local(): pl.pallas_call(functools.partial(kernel, n_seq, n_head), out_shape=jax.Sh...]
    dot_general x19 -> x0, matrix products: 105 us -> none  [the longest x4 44.3 us: span_step(): jnp.einsum('ijh,jhp->ihp', mixing, x_part, precision=lax.Precision.HIGHEST)]
    reduce_scatter x1 -> x0, waiting for transfers between devices: 87.2 us -> none  [local(): lax.psum_scatter(jnp.dot(normed, w_out, preferred_element_type=jnp.float3...]
    convert_element_type x7 -> x0, other arithmetic: 27.8 us -> none  [the longest x1 19.7 us: local(): x_heads = x_conv.astype(jnp.float32).reshape(n_rows, head_count, HEAD_DIM)]
    reshape x8 -> x0, local copies, waits for them, and re-layouts: 21.4 us -> none  [the longest x1 10.9 us: local(): outputs.reshape(n_rows, head_count, HEAD_DIM) + carried]
    another operation x9 -> x1, local copies, waits for them, and re-layouts: 14.8 us -> 0.68 us  [local(): skip = jnp.repeat(d_skip, HEAD_DIM)[None, :]]
    unnamed x1 -> x0, blocking collectives: 13.3 us -> none
  transfers between devices with their start and end apart: 4 -> 0, of which waited for: 2 -> 0; matrix products, arithmetic and copies ran while one was open for 8% -> 0% of each run, Pallas kernels for 0% -> 0%
where the time goes in v1:
time: 133 us
  Pallas kernels  125 us (94%)
  local copies, waits for them, and re-layouts  7.63 us (6%)
    pallas_call x1, Pallas kernels, local(): pl.pallas_call(functools.partial(kernel, n_seq, n_head), out_shape=jax.Sh...  125 us
    unnamed x2, local copies, waits for them, and re-layouts  5.03 us

profile of v1, /device:TPU:25, one launch (start us, length us, event | category | flops | bytes accessed | tf_op | source)
XLA Modules:
  0.0 132.8 jit_solution(11392995214117457577)
XLA Ops:
  0.0 1.2 pad_bitcast_fusion.rate_ref
  1.2 0.7 broadcast_in_dim.10
  1.9 0.7 broadcast_in_dim_reshape.3.skip_ref
  2.6 1.9 %copy.12.dt_ref = f32[1024,32]{1,0:T(8,128)} copy(f32[1024,32]{0,1:T(8,128)} %param.15) | data formatting | bytes 262144 | tf_op args[4]
  4.5 125.1 %shard_map.109 = bf16[256,4096]{1,0:T(8,128)(2,1)} custom-call(bf16[1024,2048]{1,0:T(8,128)(2,1)} %x_hbm.1, bf16[1024,2048]{1,0:T(8,128)(2,1)} %z_hbm.1, bf16[1024,128]{1,0:T(8,128)(2,1)} %b_hbm.1, bf16[1024,128]{1,0:T(8,128)(2,1)} %c_hbm.1, bf16[2048,4096]{1,0:T(8,128)(2,1)} %w_hbm.1, f32[1024,32]{1,0:T(8,128)} %copy.12.dt_ref, ...), custom_call_target="tpu_custom_call" | custom-call | flops 18790481920 | bytes 25165824 | tf_op jit(solution)/shard_map/pallas_call | solution.py:389
  129.6 3.1 %copy.14 = bf16[256,4096]{1,0:T(8,128)(2,1)} copy(bf16[256,4096]{1,0:T(8,128)(2,1)} %shard_map.109) | data formatting | bytes 4194304

commit v2 on v1

--- a/solution.py
+++ b/solution.py
@@ -19,7 +19,8 @@
 
 
 def silu(v):
-    return v / (1.0 + jnp.exp(-v))
+    half = 0.5 * v
+    return half + half * jnp.tanh(half)
 
 
 def remote(src, dst, send, recv, **where):
@@ -33,7 +34,7 @@
     x_hbm, z_hbm, b_hbm, c_hbm, w_hbm, dt_ref, rate_ref, skip_ref, cx_ref, cbc_ref, gain_ref,
     out_ref,
     x_v, z_v, w_v, bc_v, y_v, s_v, f_v, carry_in, carry_out, spread_v, pad_v, padbc_v,
-    cs_v, dt_v, cst_v, dtt_v, tot_v, dev_v, sq_v, sq_in, send_v, mid_v, recv_v,
+    cs_v, rate_v, skip_v, cst_v, dtt_v, tot_v, dev_v, sq_v, sq_in, send_v, mid_v, recv_v,
     load_sem, rim_send, rim_recv, carry_send, carry_recv, sq_send, sq_recv,
     out_send, mid_recv, fin_recv,
 ):
@@ -87,8 +88,6 @@
     of_lane = lax.broadcasted_iota(jnp.int32, (2 * LANES, chans), 1) // HEAD_DIM
     of_row = lax.broadcasted_iota(jnp.int32, (2 * LANES, chans), 0) % LANES
     spread_v[...] = jnp.where(of_lane == of_row, 1.0, 0.0).astype(jnp.bfloat16)
-    dt_v[...] = jnp.zeros_like(dt_v)
-    dt_v[:, 0:heads] = dt_ref[...]
     f_v[...] = jnp.zeros_like(f_v)
     dev_v[...] = jnp.ones_like(dev_v)
 
@@ -111,6 +110,12 @@
             total = total + taps[k : k + 1, :] * padded[5 + k : 5 + k + CHUNK, :]
         values_ref[pl.ds(start + RIM, CHUNK), :] = silu(total).astype(jnp.bfloat16)
 
+    rate_v[...] = jnp.zeros_like(rate_v)
+    rate_v[0:1, 0:heads] = skip_ref[...]
+    skip_v[...] = over_channels(rate_v[0:8, :])
+    rate_v[0:1, 0:heads] = jnp.exp(rate_ref[...])
+    rate_v[...] = rate_v[...].T
+
     for copy in loads[:3]:
         copy.wait()
 
@@ -125,17 +130,19 @@
 
         conv(x_v, pad_v, start, cx_ref)
         conv(bc_v, padbc_v, start, cbc_ref)
-        raw = dt_v[pl.ds(start, CHUNK), :]
-        dt = jnp.maximum(raw, 0.0) + jnp.log1p(jnp.exp(-jnp.abs(raw)))
-        decay = -jnp.exp(rate_ref[...]) * dt
-        running = jnp.dot(
-            jnp.where(causal, 1.0, 0.0), decay,
+        raw = dt_ref[:, pl.ds(start, CHUNK)]
+        steps = jnp.maximum(raw, 0.0) + jnp.log1p(jnp.exp(-jnp.abs(raw)))
+        across = jnp.dot(
+            -rate_v[0:heads, 0:1] * steps, jnp.where(row_id <= col_id, 1.0, 0.0),
             precision=lax.Precision.HIGHEST, preferred_element_type=jnp.float32,
         )
-        dt_v[pl.ds(start, CHUNK), :] = dt
+        of_heads = pl.ds(pl.multiple_of(c * heads, heads), heads)
+        cst_v[of_heads, :] = across
+        dtt_v[of_heads, :] = steps
+        rest = jnp.zeros((LANES - heads, CHUNK), jnp.float32)
+        running = jnp.concatenate([across, rest], axis=0).T
+        dt = jnp.concatenate([steps, rest], axis=0).T
         cs_v[pl.ds(start, CHUNK), :] = running
-        cst_v[pl.ds(start, CHUNK), :] = running.T
-        dtt_v[pl.ds(start, CHUNK), :] = dt.T
         last = running[CHUNK - 1 : CHUNK, :]
         end = over_channels(jnp.broadcast_to(jnp.exp(last), (8, LANES)))
         tot_v[pl.ds(pl.multiple_of(c * 8, 8), 8), :] = end
@@ -156,30 +163,43 @@
             carry_out.at[:, columns], carry_in.at[:, columns], carry_send.at[k], carry_recv.at[k], seq=seq + 1
         )
 
-    def within(c, _):
-        @pl.when(c == seq * chunks // n_seq)
-        def _():
-            for k in range(pieces):
-                @pl.when(seq > 0)
-                def _():
-                    carry_copy(k).wait_recv()
-
-                @pl.when(seq < n_seq - 1)
-                def _():
-                    columns = slice(k * piece, (k + 1) * piece)
-                    carry_out[:, columns] = (
-                        dev_v[0:1, columns] * carry_in[:, columns].astype(jnp.float32) + f_v[:, columns]
-                    ).astype(jnp.bfloat16)
-                    carry_copy(k).start()
-
+    def serve():
+        for k in range(pieces):
+            @pl.when(seq > 0)
+            def _():
+                carry_copy(k).wait_recv()
+
+            @pl.when(seq < n_seq - 1)
+            def _():
+                columns = slice(k * piece, (k + 1) * piece)
+                carry_out[:, columns] = (
+                    dev_v[0:1, columns] * carry_in[:, columns].astype(jnp.float32) + f_v[:, columns]
+                ).astype(jnp.bfloat16)
+                carry_copy(k).start()
+
+        f_v[...] = carry_in[...].astype(jnp.float32)
+
+        def starts(c, _):
+            here = pl.ds(pl.multiple_of(c * state, state), state)
+            update = s_v[here, :].astype(jnp.float32)
+            now = f_v[...]
+            s_v[here, :] = now.astype(jnp.bfloat16)
+            f_v[...] = now * tot_v[pl.ds(pl.multiple_of(c * 8, 8), 8), :][0:1, :] + update
+            return 0
+
+        lax.fori_loop(0, chunks, starts, 0)
+        loads[3].wait()
+
+    def within(c):
         start = pl.multiple_of(c * CHUNK, CHUNK)
         b = bc_v[pl.ds(start + RIM, CHUNK), 0:state]
         cc = bc_v[pl.ds(start + RIM, CHUNK), state : 2 * state]
         scores = lax.dot_general(cc, b, (((1,), (1,)), ((), ())), preferred_element_type=jnp.float32)
         scores = jnp.where(causal, scores, 0.0)
         running = cs_v[pl.ds(start, CHUNK), :]
-        across = cst_v[pl.ds(start, CHUNK), :]
-        steps = dtt_v[pl.ds(start, CHUNK), :]
+        of_heads = pl.ds(pl.multiple_of(c * heads, heads), heads)
+        across = cst_v[of_heads, :]
+        steps = dtt_v[of_heads, :]
         left = lax.broadcasted_iota(jnp.int32, (CHUNK, LANES), 1) < HEAD_DIM
         zero = jnp.zeros((CHUNK, LANES), jnp.bfloat16)
         for pair in range(heads // 2):
@@ -194,22 +214,6 @@
             y_v[pl.ds(start, CHUNK), lanes] = jnp.dot(
                 jnp.concatenate(mixes, axis=1), both, preferred_element_type=jnp.float32
             )
-        return 0
-
-    lax.fori_loop(0, chunks, within, 0)
-
-    f_v[...] = carry_in[...].astype(jnp.float32)
-
-    def starts(c, _):
-        here = pl.ds(pl.multiple_of(c * state, state), state)
-        update = s_v[here, :].astype(jnp.float32)
-        now = f_v[...]
-        s_v[here, :] = now.astype(jnp.bfloat16)
-        f_v[...] = now * tot_v[pl.ds(pl.multiple_of(c * 8, 8), 8), :][0:1, :] + update
-        return 0
-
-    lax.fori_loop(0, chunks, starts, 0)
-    loads[3].wait()
 
     def gate(c):
         start = pl.multiple_of(c * CHUNK, CHUNK)
@@ -220,7 +224,7 @@
             cc, s_v[pl.ds(pl.multiple_of(c * state, state), state), :], preferred_element_type=jnp.float32
         )
         x = x_v[pl.ds(start + RIM, CHUNK), :].astype(jnp.float32)
-        ssd = y_v[here, :] + earlier * grown + skip_ref[...] * x
+        ssd = y_v[here, :] + earlier * grown + skip_v[0:1, :] * x
         gated = ssd * silu(z_v[here, :].astype(jnp.float32))
         z_v[here, :] = (gated * gain_ref[...]).astype(jnp.bfloat16)
         squares = gated * gated
@@ -279,9 +283,6 @@
                 head=by_x if slot == 0 else by_y,
             )
 
-        gates(far)
-        loads[4].wait()
-
         def first(i, _):
             send_v[0, i] = product(far, i).astype(jnp.bfloat16)
             mid_copy(i, by_x).start()
@@ -289,7 +290,22 @@
             mid_copy(i + half, by_y).start()
             return 0
 
-        lax.fori_loop(0, half, first, 0)
+        turn = per_block + seq * (chunks - per_block) // n_seq
+
+        def in_order(i, _):
+            @pl.when(i == turn)
+            def _():
+                serve()
+                gates(far)
+                loads[4].wait()
+                lax.fori_loop(0, half, first, 0)
+
+            j = i // per_block
+            block = 2 * lax.rem(head // 2 + j + 1, 2) + lax.rem(lax.rem(head, 2) + 1 + j // 2, 2)
+            within(block * per_block + lax.rem(i, per_block))
+            return 0
+
+        lax.fori_loop(0, chunks, in_order, 0)
         gates(by_x)
         gates(by_y)
 
@@ -333,6 +349,15 @@
                 head=lax.rem(head + slot + 1, n_head),
             )
 
+        def in_order(c, _):
+            @pl.when(c == seq * chunks // n_seq)
+            def _():
+                serve()
+
+            within(c)
+            return 0
+
+        lax.fori_loop(0, chunks, in_order, 0)
         lax.fori_loop(0, chunks, lambda c, _: (gate(c), 0)[1], 0)
         loads[4].wait()
         for s in range(1, n_head):
@@ -376,10 +401,8 @@
     own = rows // n_head
     tiles = width // TILE
     chunks = rows // CHUNK
-    pieces = 4
+    pieces = min(8, chans // LANES)
     heads = a_log.shape[0]
-    rate = jnp.pad(a_log, (0, LANES - heads))[None, :]
-    skip = jnp.repeat(d_skip, HEAD_DIM)[None, :]
     sends, mids, slots = (3, tiles, 2) if n_head == 4 else (n_head - 1, 1, n_head - 1)
     bf, f32 = jnp.bfloat16, jnp.float32
     any_spec = pl.BlockSpec(memory_space=pl.ANY)
@@ -405,9 +428,10 @@
             pltpu.VMEM((8 + CHUNK, chans), f32),
             pltpu.VMEM((8 + CHUNK, 2 * state), f32),
             pltpu.VMEM((rows, LANES), f32),
-            pltpu.VMEM((rows, LANES), f32),
-            pltpu.VMEM((chunks * LANES, CHUNK), f32),
-            pltpu.VMEM((chunks * LANES, CHUNK), f32),
+            pltpu.VMEM((LANES, LANES), f32),
+            pltpu.VMEM((8, chans), f32),
+            pltpu.VMEM((chunks * heads, CHUNK), f32),
+            pltpu.VMEM((chunks * heads, CHUNK), f32),
             pltpu.VMEM((chunks * 8, chans), f32),
             pltpu.VMEM((8, chans), f32),
             pltpu.VMEM((rows, LANES), f32),
@@ -425,7 +449,7 @@
         cost_estimate=pl.CostEstimate(
             flops=flops, bytes_accessed=2 * (2 * rows * chans + chans * width), transcendentals=rows * chans
         ),
-    )(x_in, z_gate, b_in, c_in, w_out, dt_raw, rate, skip, conv_x, conv_bc, norm_gain[None, :])
+    )(x_in, z_gate, b_in, c_in, w_out, dt_raw.T, a_log[None, :], d_skip[None, :], conv_x, conv_bc, norm_gain[None, :])
 
 
 def solution(mesh):

time: 133 us -> 127 us (0.955)
  local copies, waits for them, and re-layouts: 7.63 us -> 3.13 us
    broadcast_in_dim x2 -> x0, local copies, waits for them, and re-layouts: 1.92 us -> none  [the longest x1 1.2 us: local(): rate = jnp.pad(a_log, (0, LANES - heads))[None, :]]
    unnamed x2 -> x1, local copies, waits for them, and re-layouts: 5.03 us -> 3.13 us
where the time goes in v2:
time: 127 us
  Pallas kernels  124 us (98%)
  local copies, waits for them, and re-layouts  3.13 us (2%)
    pallas_call x1, Pallas kernels, local(): pl.pallas_call(functools.partial(kernel, n_seq, n_head), out_shape=jax.Sh...  124 us
    unnamed x1, local copies, waits for them, and re-layouts  3.13 us

profile of v2, /device:TPU:25, one launch (start us, length us, event | category | flops | bytes accessed | tf_op | source)
XLA Modules:
  0.0 127.0 jit_solution(16435048312636884153)
XLA Ops:
  0.0 123.9 %shard_map.109 = bf16[256,4096]{1,0:T(8,128)(2,1)} custom-call(bf16[1024,2048]{1,0:T(8,128)(2,1)} %x_hbm.1, bf16[1024,2048]{1,0:T(8,128)(2,1)} %z_hbm.1, bf16[1024,128]{1,0:T(8,128)(2,1)} %b_hbm.1, bf16[1024,128]{1,0:T(8,128)(2,1)} %c_hbm.1, bf16[2048,4096]{1,0:T(8,128)(2,1)} %w_hbm.1, f32[32,1024]{1,0:T(8,128)} %bitcast.4, f32[1,32]{1,0:T(1,128)} %bitcast.6, ...), custom_call_target="tpu_custom_call" | custom-call | flops 18790481920 | bytes 25165824 | tf_op jit(solution)/shard_map/pallas_call | solution.py:412
  123.9 3.1 %copy.13 = bf16[256,4096]{1,0:T(8,128)(2,1)} copy(bf16[256,4096]{1,0:T(8,128)(2,1)} %shard_map.109) | data formatting | bytes 4194304

commit v3 on v2

--- a/solution.py
+++ b/solution.py
@@ -33,7 +33,7 @@
     n_seq, n_head,
     x_hbm, z_hbm, b_hbm, c_hbm, w_hbm, dt_ref, rate_ref, skip_ref, cx_ref, cbc_ref, gain_ref,
     out_ref,
-    x_v, z_v, w_v, bc_v, y_v, s_v, f_v, carry_in, carry_out, spread_v, pad_v, padbc_v,
+    x_v, z_v, w_v, bc_v, y_v, s_v, f_v, carry_in, carry_out, pad_v, padbc_v,
     cs_v, rate_v, skip_v, cst_v, dtt_v, tot_v, dev_v, sq_v, sq_in, send_v, mid_v, recv_v,
     load_sem, rim_send, rim_recv, carry_send, carry_recv, sq_send, sq_recv,
     out_send, mid_recv, fin_recv,
@@ -85,9 +85,6 @@
         bc_v[0:RIM, :] = jnp.zeros((RIM, 2 * state), jnp.bfloat16)
         carry_in[...] = jnp.zeros_like(carry_in)
 
-    of_lane = lax.broadcasted_iota(jnp.int32, (2 * LANES, chans), 1) // HEAD_DIM
-    of_row = lax.broadcasted_iota(jnp.int32, (2 * LANES, chans), 0) % LANES
-    spread_v[...] = jnp.where(of_lane == of_row, 1.0, 0.0).astype(jnp.bfloat16)
     f_v[...] = jnp.zeros_like(f_v)
     dev_v[...] = jnp.ones_like(dev_v)
 
@@ -95,24 +92,28 @@
     col_id = lax.broadcasted_iota(jnp.int32, (CHUNK, CHUNK), 1)
     causal = row_id >= col_id
 
-    def over_channels(values):
-        high = values.astype(jnp.bfloat16)
-        low = (values - high.astype(jnp.float32)).astype(jnp.bfloat16)
-        return jnp.dot(
-            jnp.concatenate([high, low], axis=1), spread_v[...], preferred_element_type=jnp.float32
+    left = lax.broadcasted_iota(jnp.int32, (CHUNK, LANES), 1) < HEAD_DIM
+    groups = [slice(g, g + LANES) for g in range(0, chans, LANES)]
+
+    def over_channels(values, g):
+        return jnp.where(
+            left[0 : values.shape[0]], values[:, 2 * g : 2 * g + 1], values[:, 2 * g + 1 : 2 * g + 2]
         )
 
-    def conv(values_ref, padded, start, taps):
-        padded[0:8, :] = values_ref[pl.ds(start, RIM), :].astype(jnp.float32)[8:16]
-        padded[8 : 8 + CHUNK, :] = values_ref[pl.ds(start + RIM, CHUNK), :].astype(jnp.float32)
-        total = taps[0:1, :] * padded[5 : 5 + CHUNK, :]
+    def conv(values_ref, padded, start, taps, lanes):
+        padded[0:8, lanes] = values_ref[pl.ds(start, RIM), lanes].astype(jnp.float32)[8:16]
+        padded[8 : 8 + CHUNK, lanes] = values_ref[pl.ds(start + RIM, CHUNK), lanes].astype(jnp.float32)
+        total = taps[0:1, lanes] * padded[5 : 5 + CHUNK, lanes]
         for k in range(1, 4):
-            total = total + taps[k : k + 1, :] * padded[5 + k : 5 + k + CHUNK, :]
-        values_ref[pl.ds(start + RIM, CHUNK), :] = silu(total).astype(jnp.bfloat16)
+            total = total + taps[k : k + 1, lanes] * padded[5 + k : 5 + k + CHUNK, lanes]
+        result = silu(total).astype(jnp.bfloat16)
+        values_ref[pl.ds(start + RIM, CHUNK), lanes] = result
+        return result
 
     rate_v[...] = jnp.zeros_like(rate_v)
     rate_v[0:1, 0:heads] = skip_ref[...]
-    skip_v[...] = over_channels(rate_v[0:8, :])
+    for g, lanes in enumerate(groups):
+        skip_v[:, lanes] = over_channels(rate_v[0:8, :], g)
     rate_v[0:1, 0:heads] = jnp.exp(rate_ref[...])
     rate_v[...] = rate_v[...].T
 
@@ -128,8 +129,8 @@
             for copy in rims:
                 copy.wait_recv()
 
-        conv(x_v, pad_v, start, cx_ref)
-        conv(bc_v, padbc_v, start, cbc_ref)
+        for g in range(0, 2 * state, LANES):
+            conv(bc_v, padbc_v, start, cbc_ref, slice(g, g + LANES))
         raw = dt_ref[:, pl.ds(start, CHUNK)]
         steps = jnp.maximum(raw, 0.0) + jnp.log1p(jnp.exp(-jnp.abs(raw)))
         across = jnp.dot(
@@ -144,15 +145,22 @@
         dt = jnp.concatenate([steps, rest], axis=0).T
         cs_v[pl.ds(start, CHUNK), :] = running
         last = running[CHUNK - 1 : CHUNK, :]
-        end = over_channels(jnp.broadcast_to(jnp.exp(last), (8, LANES)))
-        tot_v[pl.ds(pl.multiple_of(c * 8, 8), 8), :] = end
-        weights = over_channels(jnp.exp(last - running) * dt)
-        xw = (weights * x_v[pl.ds(start + RIM, CHUNK), :].astype(jnp.float32)).astype(jnp.bfloat16)
+        end = jnp.broadcast_to(jnp.exp(last), (8, LANES))
+        weights = jnp.exp(last - running) * dt
         b_t = bc_v[pl.ds(start + RIM, CHUNK), 0:state].astype(jnp.float32).T.astype(jnp.bfloat16)
-        update = jnp.dot(b_t, xw, preferred_element_type=jnp.float32)
-        s_v[pl.ds(pl.multiple_of(c * state, state), state), :] = update.astype(jnp.bfloat16)
-        f_v[...] += dev_v[0:1, :] * update
-        dev_v[...] = dev_v[...] * end
+        ends = pl.ds(pl.multiple_of(c * 8, 8), 8)
+        here = pl.ds(pl.multiple_of(c * state, state), state)
+        for g in range(0, len(groups), 2):
+            weighted = []
+            for one in (g, g + 1):
+                x = conv(x_v, pad_v, start, cx_ref, groups[one])
+                tot_v[ends, groups[one]] = over_channels(end, one)
+                weighted.append((over_channels(weights, one) * x.astype(jnp.float32)).astype(jnp.bfloat16))
+            update = jnp.dot(b_t, jnp.concatenate(weighted, axis=1), preferred_element_type=jnp.float32)
+            both = slice(g * LANES, (g + 2) * LANES)
+            s_v[here, both] = update.astype(jnp.bfloat16)
+            f_v[:, both] += dev_v[0:1, both] * update
+            dev_v[:, both] = dev_v[:, both] * tot_v[ends, both]
         return 0
 
     lax.fori_loop(0, chunks, state_step, 0)
@@ -181,10 +189,12 @@
 
         def starts(c, _):
             here = pl.ds(pl.multiple_of(c * state, state), state)
-            update = s_v[here, :].astype(jnp.float32)
-            now = f_v[...]
-            s_v[here, :] = now.astype(jnp.bfloat16)
-            f_v[...] = now * tot_v[pl.ds(pl.multiple_of(c * 8, 8), 8), :][0:1, :] + update
+            ends = pl.ds(pl.multiple_of(c * 8, 8), 8)
+            for lanes in groups:
+                update = s_v[here, lanes].astype(jnp.float32)
+                now = f_v[:, lanes]
+                s_v[here, lanes] = now.astype(jnp.bfloat16)
+                f_v[:, lanes] = now * tot_v[ends, lanes][0:1, :] + update
             return 0
 
         lax.fori_loop(0, chunks, starts, 0)
@@ -200,7 +210,6 @@
         of_heads = pl.ds(pl.multiple_of(c * heads, heads), heads)
         across = cst_v[of_heads, :]
         steps = dtt_v[of_heads, :]
-        left = lax.broadcasted_iota(jnp.int32, (CHUNK, LANES), 1) < HEAD_DIM
         zero = jnp.zeros((CHUNK, LANES), jnp.bfloat16)
         for pair in range(heads // 2):
             mixes = []
@@ -219,18 +228,20 @@
         start = pl.multiple_of(c * CHUNK, CHUNK)
         here = pl.ds(start, CHUNK)
         cc = bc_v[pl.ds(start + RIM, CHUNK), state : 2 * state]
-        grown = over_channels(jnp.exp(cs_v[here, :]))
-        earlier = jnp.dot(
-            cc, s_v[pl.ds(pl.multiple_of(c * state, state), state), :], preferred_element_type=jnp.float32
-        )
-        x = x_v[pl.ds(start + RIM, CHUNK), :].astype(jnp.float32)
-        ssd = y_v[here, :] + earlier * grown + skip_v[0:1, :] * x
-        gated = ssd * silu(z_v[here, :].astype(jnp.float32))
-        z_v[here, :] = (gated * gain_ref[...]).astype(jnp.bfloat16)
-        squares = gated * gated
-        total = squares[:, 0:LANES]
-        for g in range(1, chans // LANES):
-            total = total + squares[:, g * LANES : (g + 1) * LANES]
+        grown = jnp.exp(cs_v[here, :])
+        states = pl.ds(pl.multiple_of(c * state, state), state)
+        total = jnp.zeros((CHUNK, LANES), jnp.float32)
+        for g in range(0, len(groups), 2):
+            both = slice(g * LANES, (g + 2) * LANES)
+            earlier = jnp.dot(cc, s_v[states, both], preferred_element_type=jnp.float32)
+            for one in (g, g + 1):
+                lanes = groups[one]
+                part = earlier[:, (one - g) * LANES : (one - g + 1) * LANES] * over_channels(grown, one)
+                x = x_v[pl.ds(start + RIM, CHUNK), lanes].astype(jnp.float32)
+                ssd = y_v[here, lanes] + part + skip_v[0:1, lanes] * x
+                gated = ssd * silu(z_v[here, lanes].astype(jnp.float32))
+                z_v[here, lanes] = (gated * gain_ref[:, lanes]).astype(jnp.bfloat16)
+                total = total + gated * gated
         sq_v[here, :] = total
 
     def product(block, t):
@@ -424,7 +435,6 @@
             pltpu.VMEM((state, chans), f32),
             pltpu.VMEM((state, chans), bf),
             pltpu.VMEM((state, chans), bf),
-            pltpu.VMEM((2 * LANES, chans), bf),
             pltpu.VMEM((8 + CHUNK, chans), f32),
             pltpu.VMEM((8 + CHUNK, 2 * state), f32),
             pltpu.VMEM((rows, LANES), f32),

time: 127 us -> 128 us (level)
    pallas_call x1, Pallas kernels: 124 us -> 125 us  [local(): pl.pallas_call(functools.partial(kernel, n_seq, n_head), out_shape=jax.Sh...]
where the time goes in v3:
time: 128 us
  Pallas kernels  125 us (98%)
  local copies, waits for them, and re-layouts  3.13 us (2%)
    pallas_call x1, Pallas kernels, local(): pl.pallas_call(functools.partial(kernel, n_seq, n_head), out_shape=jax.Sh...  125 us
    unnamed x1, local copies, waits for them, and re-layouts  3.13 us

profile of v3, /device:TPU:25, one launch (start us, length us, event | category | flops | bytes accessed | tf_op | source)
XLA Modules:
  0.0 128.3 jit_solution(8166603157802779119)
XLA Ops:
  0.0 125.1 %shard_map.109 = bf16[256,4096]{1,0:T(8,128)(2,1)} custom-call(bf16[1024,2048]{1,0:T(8,128)(2,1)} %x_hbm.1, bf16[1024,2048]{1,0:T(8,128)(2,1)} %z_hbm.1, bf16[1024,128]{1,0:T(8,128)(2,1)} %b_hbm.1, bf16[1024,128]{1,0:T(8,128)(2,1)} %c_hbm.1, bf16[2048,4096]{1,0:T(8,128)(2,1)} %w_hbm.1, f32[32,1024]{1,0:T(8,128)} %bitcast.4, f32[1,32]{1,0:T(1,128)} %bitcast.6, ...), custom_call_target="tpu_custom_call" | custom-call | flops 18790481920 | bytes 25165824 | tf_op jit(solution)/shard_map/pallas_call | solution.py:423
  125.1 3.1 %copy.13 = bf16[256,4096]{1,0:T(8,128)(2,1)} copy(bf16[256,4096]{1,0:T(8,128)(2,1)} %shard_map.109) | data formatting | bytes 4194304
